TPU v7x, 256 devices: a whole 4x4x8 slice. The times are simulated.
256 devices in a mesh: dom: 64 (over x, z, core), sub: 4 (over y).
Axes of the slice: x: 4, y: 4, z: 8, core: 2. Of those that a mesh axis runs over, the one named last changes fastest.
Arguments:
- positions: float32 [3, 2097152], P(None, ('dom', 'sub')), may hold values from 0 to 1
- masses: float32 [2097152], P(('dom', 'sub')), may hold values from 0.00029296876 to 0.0029296875
- cell_mass: float32 [32768], P(('dom', 'sub')), may hold values from 0.00234375 to 0.0234375
- cell_center: float32 [3, 32768], P(None, ('dom', 'sub')), may hold values from 0 to 1
- cell_quad: float32 [6, 32768], P(None, ('dom', 'sub')), may hold values from -0.0046875 to 0.0046875
- cell_list: int32 [32768, 128], P(('dom', 'sub')), may hold values from 0 to 32767
- leaf_list: int32 [32768, 16], P(('dom', 'sub')), may hold values from 0 to 575, as said below
- send_list: int32 [64, 4, 8, 8], P('dom', 'sub'), may hold values from 0 to 127
- send_count: int32 [64, 4, 8], P('dom', 'sub'), may hold values from 1 to 8, as said below
Outputs:
- accel: float32 [3, 2097152], P(None, ('dom', 'sub'))
Inputs may be any that keep to these rules, and one draw needn't show every extreme that they name: `send_count`: counts fall off with the distance along the curve: an offset of one domain always carries 8 blocks, an offset of d domains at most max(1, 8 // d). `leaf_list`: each id names a block of the group's own domain or a slot of the far part that carries a block.
All inputs are finite; a program needn't handle non-finite values.
Results may differ from a plain program's by a relative error of at most 0.0003.
Values sent between devices are 32-bit elements; how exact they have to be, the bound alone decides.
A program may use at most 128 MiB of HBM per device.

v0:
```python
import jax
import jax.numpy as jnp
from jax import lax
from jax.sharding import PartitionSpec as P

LEAF = 64
LEAF_DEV = 128
NCELL = 128
NLEAF = 16
RANGE = 4
CAP = 8
softening_sq = 0.0025


def passed_along(value, axis, steps):
    count = lax.axis_size(axis)
    leading, last = (max(0, -steps), min(count, count - steps))
    return lax.ppermute(value, axis, [(source, source + steps) for source in range(leading, last)])


def direct_pull(targets, sources, weights):
    offset = sources[:, :, None, :] - targets[:, :, :, None]
    dist_sq = jnp.sum(offset * offset, axis=0) + softening_sq
    factor = weights[:, None, :] / (dist_sq * jnp.sqrt(dist_sq))
    return jnp.sum(offset * factor[None], axis=-1)


def multipole_pull(targets, moments):
    offset = targets[:, :, :, None] - moments[1:4, :, None, :]
    dist_sq = jnp.sum(offset * offset, axis=0) + softening_sq
    inv_one = 1.0 / jnp.sqrt(dist_sq)
    inv_two = inv_one * inv_one
    inv_three = inv_one * inv_two
    inv_five = inv_three * inv_two
    inv_seven = inv_five * inv_two
    quad_part = moments[4:10, :, None, :]
    q_times_x = quad_part[0] * offset[0] + quad_part[3] * offset[1] + quad_part[4] * offset[2]
    q_times_y = quad_part[3] * offset[0] + quad_part[1] * offset[1] + quad_part[5] * offset[2]
    q_times_z = quad_part[4] * offset[0] + quad_part[5] * offset[1] + quad_part[2] * offset[2]
    q_times = jnp.stack([q_times_x, q_times_y, q_times_z])
    quad_form = jnp.sum(offset * q_times, axis=0)
    mass_part = moments[0, :, None, :]
    accel_terms = (
        -mass_part * inv_three * offset + inv_five * q_times - 2.5 * inv_seven * quad_form * offset
    )
    return jnp.sum(accel_terms, axis=-1)


def group_pull(targets, essential, leaf_ids, cell_table, cell_ids):
    groups_here = leaf_ids.shape[0]
    particle_ids = (
        leaf_ids[:, :, None] * LEAF + jnp.arange(LEAF, dtype=jnp.int32)[None, None, :]
    ).reshape(groups_here, -1)
    picked = essential[:, particle_ids]
    moments = cell_table[:, cell_ids]
    return direct_pull(targets, picked[0:3], picked[3]) + multipole_pull(targets, moments)


def on_device(
    positions,
    masses,
    cell_mass,
    cell_center,
    cell_quad,
    cell_list,
    leaf_list,
    send_list,
    send_count,
):
    offset_values = list(range(-RANGE, 0)) + list(range(1, RANGE + 1))
    cell_table = jnp.concatenate([cell_mass[None], cell_center, cell_quad], axis=0)
    all_cells = lax.all_gather(cell_table, ("dom", "sub"), axis=1, tiled=True)
    packed = jnp.concatenate([positions, masses[None]], axis=0)
    nearby = lax.all_gather(packed, "sub", axis=1, tiled=True)
    chosen = send_list.reshape(2 * RANGE, CAP)
    counts = send_count.reshape(2 * RANGE)
    live = (jnp.arange(CAP, dtype=jnp.int32)[None, :] < counts[:, None]).astype(jnp.float32)
    weight = jnp.repeat(live.reshape(-1), LEAF).reshape(2 * RANGE, CAP * LEAF)
    flat_ids = (
        chosen[:, :, None] * LEAF + jnp.arange(LEAF, dtype=jnp.int32)[None, None, :]
    ).reshape(2 * RANGE, CAP * LEAF)
    outgoing = packed[:, flat_ids] * weight[None]
    pieces = []
    for slot in range(2 * RANGE):
        pieces.append(passed_along(outgoing[:, slot], "dom", offset_values[slot]))
    remote = jnp.stack(pieces, axis=1)
    essential = jnp.concatenate([nearby, remote.reshape(4, 2 * RANGE * CAP * LEAF)], axis=1)
    block_size = 8
    block_count = LEAF_DEV // block_size
    target_blocks = positions.reshape(3, block_count, block_size, LEAF).transpose(1, 0, 2, 3)
    leaf_blocks = leaf_list.reshape(block_count, block_size, NLEAF)
    cell_blocks = cell_list.reshape(block_count, block_size, NCELL)

    def one_block(inputs):
        block_targets, block_leaves, block_cells = inputs
        return group_pull(block_targets, essential, block_leaves, all_cells, block_cells)

    pulled = lax.map(one_block, (target_blocks, leaf_blocks, cell_blocks))
    return pulled.transpose(1, 0, 2, 3).reshape(3, LEAF_DEV * LEAF)


def solution(mesh):
    return jax.shard_map(
        on_device,
        mesh=mesh,
        in_specs=(
            P(None, ("dom", "sub")),
            P(("dom", "sub")),
            P(("dom", "sub")),
            P(None, ("dom", "sub")),
            P(None, ("dom", "sub")),
            P(("dom", "sub"), None),
            P(("dom", "sub"), None),
            P("dom", "sub", None, None),
            P("dom", "sub", None),
        ),
        out_specs=P(None, ("dom", "sub")),
        check_vma=False,
    )
```

profile of v0, /device:TPU:1, one launch (start us, length us, event | category | flops | bytes accessed | tf_op | source)
XLA Modules:
  0.0 975.4 jit_solution(4220310291080115131)
XLA Ops:
  10.5 12.9 %gather_fusion.2 = f32[4096,4]{1,0:T(8,128)S(1)} fusion(f32[4,8192]{0,1:T(8,128)} %copy.47, s32[4096]{0:T(1024)S(1)} %broadcast_clamp_fusion), kind=kCustom, calls=%fused_computation.2 | custom fusion | bytes 147456 | tf_op jit(solution)/shard_map/gather | solution.py:82
  52.1 10.8 %all_gather.6 = f32[4,32768]{1,0:T(4,128)S(1)} all-gather(f32[4,8192]{1,0:T(4,128)S(1)} %pad_maximum_fusion.2), channel_id=1, replica_groups=mesh['dom'=64,'sub'=4] {'sub'}, dimensions={1}, use_global_device_ids=true | all-gather | bytes 655360 | tf_op jit(solution)/shard_map/all_gather | solution.py:74
  63.7 9.8 %copy.56 = f32[4,36864]{0,1:T(8,128)} copy(f32[4,36864]{1,0:T(4,128)S(1)} %pad_maximum_fusion.1) | data formatting | bytes 1179648 | tf_op jit(solution)/shard_map/while | solution.py:98
  73.5 75.3 %all-gather.2.cloned.1.call-done = f32[10,32768]{1,0:T(8,128)} async-done(((f32[10,128]{1,0:T(8,128)}), f32[10,32768]{1,0:T(8,128)}) %all-gather.2.cloned.1.call-update) | async-done | bytes 1310736 | tf_op jit(solution)/shard_map/all_gather | solution.py:72
  148.8 9.7 copy.58
  158.5 809.3 %while.10 = (s32[]{:T(128)}, f32[16,3,8,64]{3,2,1,0:T(8,128)S(1)}, s32[16,8,16]{2,1,0:T(8,128)S(1)}, f32[4,36864]{0,1:T(8,128)}, f32[16,3,8,64]{3,2,0,1:T(8,128)...) while((s32[]{:T(128)}, f32[16,3,8,64]{3,2,1,0:T(8,128)S(1)}, s32[16,8,16]{2,1,0:T(8,128)S(1)}, ...), condition=%wide.region_6.7_spmd, body=%wide.region_0.6_spmd.sunk | while | flops 15249026 | bytes 16653933 | solution.py:98
  158.8 34.1 %gather_fusion = f32[8192,4]{1,0:T(8,128)} fusion(f32[4,36864]{0,1:T(8,128)} %get-tuple-element.193, s32[8192]{0:T(1024)S(1)} %bitcast_clamp_fusion.2), kind=kCustom, calls=%fused_computation.clone.1 | custom fusion | bytes 294912 | tf_op jit(solution)/shard_map/while/body/eval_jaxpr/gather | solution.py:54
  209.4 34.1 %gather_fusion = f32[8192,4]{1,0:T(8,128)} fusion(f32[4,36864]{0,1:T(8,128)} %get-tuple-element.193, s32[8192]{0:T(1024)S(1)} %bitcast_clamp_fusion.2), kind=kCustom, calls=%fused_computation.clone.1 | custom fusion | bytes 294912 | tf_op jit(solution)/shard_map/while/body/eval_jaxpr/gather | solution.py:54
  259.9 34.1 %gather_fusion = f32[8192,4]{1,0:T(8,128)} fusion(f32[4,36864]{0,1:T(8,128)} %get-tuple-element.193, s32[8192]{0:T(1024)S(1)} %bitcast_clamp_fusion.2), kind=kCustom, calls=%fused_computation.clone.1 | custom fusion | bytes 294912 | tf_op jit(solution)/shard_map/while/body/eval_jaxpr/gather | solution.py:54
  310.5 34.1 %gather_fusion = f32[8192,4]{1,0:T(8,128)} fusion(f32[4,36864]{0,1:T(8,128)} %get-tuple-element.193, s32[8192]{0:T(1024)S(1)} %bitcast_clamp_fusion.2), kind=kCustom, calls=%fused_computation.clone.1 | custom fusion | bytes 294912 | tf_op jit(solution)/shard_map/while/body/eval_jaxpr/gather | solution.py:54
  361.1 34.1 %gather_fusion = f32[8192,4]{1,0:T(8,128)} fusion(f32[4,36864]{0,1:T(8,128)} %get-tuple-element.193, s32[8192]{0:T(1024)S(1)} %bitcast_clamp_fusion.2), kind=kCustom, calls=%fused_computation.clone.1 | custom fusion | bytes 294912 | tf_op jit(solution)/shard_map/while/body/eval_jaxpr/gather | solution.py:54
  411.7 34.1 %gather_fusion = f32[8192,4]{1,0:T(8,128)} fusion(f32[4,36864]{0,1:T(8,128)} %get-tuple-element.193, s32[8192]{0:T(1024)S(1)} %bitcast_clamp_fusion.2), kind=kCustom, calls=%fused_computation.clone.1 | custom fusion | bytes 294912 | tf_op jit(solution)/shard_map/while/body/eval_jaxpr/gather | solution.py:54
  451.7 8.6 gather_fusion.1
  462.3 34.1 %gather_fusion = f32[8192,4]{1,0:T(8,128)} fusion(f32[4,36864]{0,1:T(8,128)} %get-tuple-element.193, s32[8192]{0:T(1024)S(1)} %bitcast_clamp_fusion.2), kind=kCustom, calls=%fused_computation.clone.1 | custom fusion | bytes 294912 | tf_op jit(solution)/shard_map/while/body/eval_jaxpr/gather | solution.py:54
  512.8 34.1 %gather_fusion = f32[8192,4]{1,0:T(8,128)} fusion(f32[4,36864]{0,1:T(8,128)} %get-tuple-element.193, s32[8192]{0:T(1024)S(1)} %bitcast_clamp_fusion.2), kind=kCustom, calls=%fused_computation.clone.1 | custom fusion | bytes 294912 | tf_op jit(solution)/shard_map/while/body/eval_jaxpr/gather | solution.py:54
  563.4 34.1 %gather_fusion = f32[8192,4]{1,0:T(8,128)} fusion(f32[4,36864]{0,1:T(8,128)} %get-tuple-element.193, s32[8192]{0:T(1024)S(1)} %bitcast_clamp_fusion.2), kind=kCustom, calls=%fused_computation.clone.1 | custom fusion | bytes 294912 | tf_op jit(solution)/shard_map/while/body/eval_jaxpr/gather | solution.py:54
  614.0 34.1 %gather_fusion = f32[8192,4]{1,0:T(8,128)} fusion(f32[4,36864]{0,1:T(8,128)} %get-tuple-element.193, s32[8192]{0:T(1024)S(1)} %bitcast_clamp_fusion.2), kind=kCustom, calls=%fused_computation.clone.1 | custom fusion | bytes 294912 | tf_op jit(solution)/shard_map/while/body/eval_jaxpr/gather | solution.py:54
  664.6 34.1 %gather_fusion = f32[8192,4]{1,0:T(8,128)} fusion(f32[4,36864]{0,1:T(8,128)} %get-tuple-element.193, s32[8192]{0:T(1024)S(1)} %bitcast_clamp_fusion.2), kind=kCustom, calls=%fused_computation.clone.1 | custom fusion | bytes 294912 | tf_op jit(solution)/shard_map/while/body/eval_jaxpr/gather | solution.py:54
  715.2 34.1 %gather_fusion = f32[8192,4]{1,0:T(8,128)} fusion(f32[4,36864]{0,1:T(8,128)} %get-tuple-element.193, s32[8192]{0:T(1024)S(1)} %bitcast_clamp_fusion.2), kind=kCustom, calls=%fused_computation.clone.1 | custom fusion | bytes 294912 | tf_op jit(solution)/shard_map/while/body/eval_jaxpr/gather | solution.py:54
  765.7 34.1 %gather_fusion = f32[8192,4]{1,0:T(8,128)} fusion(f32[4,36864]{0,1:T(8,128)} %get-tuple-element.193, s32[8192]{0:T(1024)S(1)} %bitcast_clamp_fusion.2), kind=kCustom, calls=%fused_computation.clone.1 | custom fusion | bytes 294912 | tf_op jit(solution)/shard_map/while/body/eval_jaxpr/gather | solution.py:54
  805.8 8.6 gather_fusion.1
  816.3 34.1 %gather_fusion = f32[8192,4]{1,0:T(8,128)} fusion(f32[4,36864]{0,1:T(8,128)} %get-tuple-element.193, s32[8192]{0:T(1024)S(1)} %bitcast_clamp_fusion.2), kind=kCustom, calls=%fused_computation.clone.1 | custom fusion | bytes 294912 | tf_op jit(solution)/shard_map/while/body/eval_jaxpr/gather | solution.py:54
  866.9 34.1 %gather_fusion = f32[8192,4]{1,0:T(8,128)} fusion(f32[4,36864]{0,1:T(8,128)} %get-tuple-element.193, s32[8192]{0:T(1024)S(1)} %bitcast_clamp_fusion.2), kind=kCustom, calls=%fused_computation.clone.1 | custom fusion | bytes 294912 | tf_op jit(solution)/shard_map/while/body/eval_jaxpr/gather | solution.py:54
  917.5 34.1 %gather_fusion = f32[8192,4]{1,0:T(8,128)} fusion(f32[4,36864]{0,1:T(8,128)} %get-tuple-element.193, s32[8192]{0:T(1024)S(1)} %bitcast_clamp_fusion.2), kind=kCustom, calls=%fused_computation.clone.1 | custom fusion | bytes 294912 | tf_op jit(solution)/shard_map/while/body/eval_jaxpr/gather | solution.py:54
  (463 shorter events, 277.3 us)
Async XLA Ops:
  6.5 3.7 copy-start.2
  6.5 17.6 %copy-start.5 = (s32[1,1,8]{2,1,0:T(1,128)S(1)}, s32[1,1,8]{2,1,0:T(1,128)}, u32[]{:S(2)}) copy-start(s32[1,1,8]{2,1,0:T(1,128)} %param.19) | copy-start | bytes 100
  6.5 31.1 %copy-start.3 = (f32[6,128]{1,0:T(8,128)S(1)}, f32[6,128]{1,0:T(8,128)}, u32[]{:S(2)}) copy-start(f32[6,128]{1,0:T(8,128)} %param.15) | copy-start | bytes 9220
  6.5 31.1 %copy-start.4 = (f32[3,128]{1,0:T(4,128)S(1)}, f32[3,128]{1,0:T(4,128)}, u32[]{:S(2)}) copy-start(f32[3,128]{1,0:T(4,128)} %param.14) | copy-start | bytes 4612
  6.5 31.1 %copy-start.6 = (f32[128]{0:T(128)S(1)}, f32[128]{0:T(128)}, u32[]{:S(2)}) copy-start(f32[128]{0:T(128)} %param.13) | copy-start | bytes 1540
  6.5 142.3 %all-gather.2.cloned.1.call-start = ((), (), s32[]{:S(2)}) async-start(), calls=%async_computation | async-start | bytes 2105344 | tf_op jit(solution)/shard_map/all_gather | solution.py:72
  7.6 55.3 %copy-start = (f32[3,8192]{1,0:T(4,128)S(1)}, f32[3,8192]{1,0:T(4,128)}, u32[]{:S(2)}) copy-start(f32[3,8192]{1,0:T(4,128)} %param.11) | copy-start | bytes 294916
  7.6 55.5 %copy-start.1 = (s32[128,16]{0,1:T(8,128)S(1)}, s32[128,16]{0,1:T(8,128)}, u32[]{:S(2)}) copy-start(s32[128,16]{0,1:T(8,128)} %param.17) | copy-start | bytes 24580
  24.4 13.9 %collective-permute-start = (f32[4,512]{1,0:T(4,128)S(1)}, f32[4,512]{1,0:T(4,128)S(1)}, u32[]{:S(2)}, u32[]{:S(2)}) collective-permute-start(f32[4,512]{1,0:T(4,128)S(1)} %get-tuple-element.100), channel_id=1, source_target_pairs={{16,0},{20,4},{24,8},{28,12},{32,16},{36,20},{40,24},{44,28},{48,3... | collective-permute-start | bytes 24584 | tf_op jit(solution)/shard_map/ppermute | solution.py:18
  25.7 17.0 %collective-permute-start.1 = (f32[4,512]{1,0:T(4,128)S(1)}, f32[4,512]{1,0:T(4,128)S(1)}, u32[]{:S(2)}, u32[]{:S(2)}) collective-permute-start(f32[4,512]{1,0:T(4,128)S(1)} %get-tuple-element.99), channel_id=1, source_target_pairs={{12,0},{16,4},{20,8},{24,12},{28,16},{32,20},{36,24},{40,28},{44,3... | collective-permute-start | bytes 24584 | tf_op jit(solution)/shard_map/ppermute | solution.py:18
  27.0 19.8 %collective-permute-start.2 = (f32[4,512]{1,0:T(4,128)S(1)}, f32[4,512]{1,0:T(4,128)S(1)}, u32[]{:S(2)}, u32[]{:S(2)}) collective-permute-start(f32[4,512]{1,0:T(4,128)S(1)} %get-tuple-element.98), channel_id=1, source_target_pairs={{8,0},{12,4},{16,8},{20,12},{24,16},{28,20},{32,24},{36,28},{40,32... | collective-permute-start | bytes 24584 | tf_op jit(solution)/shard_map/ppermute | solution.py:18
  28.3 34.9 %collective-permute-start.3 = (f32[4,512]{1,0:T(4,128)S(1)}, f32[4,512]{1,0:T(4,128)S(1)}, u32[]{:S(2)}, u32[]{:S(2)}) collective-permute-start(f32[4,512]{1,0:T(4,128)S(1)} %get-tuple-element.97), channel_id=1, source_target_pairs={{4,0},{8,4},{12,8},{16,12},{20,16},{24,20},{28,24},{32,28},{36,32}... | collective-permute-start | bytes 24584 | tf_op jit(solution)/shard_map/ppermute | solution.py:18
  33.5 29.8 %collective-permute-start.4 = (f32[4,512]{1,0:T(4,128)S(1)}, f32[4,512]{1,0:T(4,128)S(1)}, u32[]{:S(2)}, u32[]{:S(2)}) collective-permute-start(f32[4,512]{1,0:T(4,128)S(1)} %get-tuple-element.96), channel_id=1, source_target_pairs={{0,4},{4,8},{8,12},{12,16},{16,20},{20,24},{24,28},{28,32},{32,36}... | collective-permute-start | bytes 24584 | tf_op jit(solution)/shard_map/ppermute | solution.py:18
  38.3 25.0 %collective-permute-start.5 = (f32[4,512]{1,0:T(4,128)S(1)}, f32[4,512]{1,0:T(4,128)S(1)}, u32[]{:S(2)}, u32[]{:S(2)}) collective-permute-start(f32[4,512]{1,0:T(4,128)S(1)} %get-tuple-element.95), channel_id=1, source_target_pairs={{0,8},{4,12},{8,16},{12,20},{16,24},{20,28},{24,32},{28,36},{32,40... | collective-permute-start | bytes 24584 | tf_op jit(solution)/shard_map/ppermute | solution.py:18
  42.7 20.7 %collective-permute-start.6 = (f32[4,512]{1,0:T(4,128)S(1)}, f32[4,512]{1,0:T(4,128)S(1)}, u32[]{:S(2)}, u32[]{:S(2)}) collective-permute-start(f32[4,512]{1,0:T(4,128)S(1)} %get-tuple-element.94), channel_id=1, source_target_pairs={{0,12},{4,16},{8,20},{12,24},{16,28},{20,32},{24,36},{28,40},{32,4... | collective-permute-start | bytes 24584 | tf_op jit(solution)/shard_map/ppermute | solution.py:18
  46.8 16.5 %collective-permute-start.7 = (f32[4,512]{1,0:T(4,128)S(1)}, f32[4,512]{1,0:T(4,128)S(1)}, u32[]{:S(2)}, u32[]{:S(2)}) collective-permute-start(f32[4,512]{1,0:T(4,128)S(1)} %get-tuple-element.93), channel_id=1, source_target_pairs={{0,16},{4,20},{8,24},{12,28},{16,32},{20,36},{24,40},{28,44},{32,4... | collective-permute-start | bytes 24584 | tf_op jit(solution)/shard_map/ppermute | solution.py:18
Sparse Core Ops, SparseCore 0:
  38.4 110.3 all-gather.1
where the time goes:
time: 978 us; the launch traced here: 975 us
  local copies, waits for them, and re-layouts  774 us (79%)
  waiting for transfers between devices  75.3 us (8%)
  other arithmetic  72.5 us (7%)
  starting transfers between devices  27 us (3%)
  between operations  13.7 us (1%)
  blocking collectives  10.8 us (1%)
    gather x32, local copies, waits for them, and re-layouts, group_pull(): picked = essential[:, particle_ids]  592 us
    gather x32, local copies, waits for them, and re-layouts, group_pull(): moments = cell_table[:, cell_ids]  140 us
    all_gather x1, waiting for transfers between devices, on_device(): all_cells = lax.all_gather(cell_table, ('dom', 'sub'), axis=1, tiled=True)  75.3 us
    ppermute x8, starting transfers between devices, passed_along(): lax.ppermute(value, axis, [(source, source + steps) for source in range(l...  27 us
  transfers between devices with their start and end apart: 9, of which 1 were waited for; matrix products, arithmetic and copies ran while one was open for 1% of the time, Pallas kernels for 0%

commit v1 on v0

--- a/solution.py
+++ b/solution.py
@@ -69,7 +69,12 @@
 ):
     offset_values = list(range(-RANGE, 0)) + list(range(1, RANGE + 1))
     cell_table = jnp.concatenate([cell_mass[None], cell_center, cell_quad], axis=0)
-    all_cells = lax.all_gather(cell_table, ("dom", "sub"), axis=1, tiled=True)
+    all_cells = jnp.concatenate(
+        lax.all_to_all(
+            jnp.stack([cell_table] * lax.axis_size(("dom", "sub"))), ("dom", "sub"), 0, 0
+        ),
+        axis=1,
+    )
     packed = jnp.concatenate([positions, masses[None]], axis=0)
     nearby = lax.all_gather(packed, "sub", axis=1, tiled=True)
     chosen = send_list.reshape(2 * RANGE, CAP)

time: 978 us -> 930 us (0.951)
  waiting for transfers between devices: 75.3 us -> 17.8 us
  starting transfers between devices: 27 us -> 44 us
  between operations: 13.7 us -> 0.3 us
    all_gather x1 -> x0, waiting for transfers between devices: 75.3 us -> none  [on_device(): all_cells = lax.all_gather(cell_table, ('dom', 'sub'), axis=1, tiled=True)]
    all_to_all x0 -> x1, starting transfers between devices: none -> 17.5 us  [on_device(): lax.all_to_all(jnp.stack([cell_table] * lax.axis_size(('dom', 'sub'))), (...]
  transfers between devices with their start and end apart: 9 -> 9, of which waited for: 1 -> 4; matrix products, arithmetic and copies ran while one was open for 1% -> 1% of each run, Pallas kernels for 0% -> 0%
where the time goes in v1:
time: 930 us; the launch traced here: 924 us
  local copies, waits for them, and re-layouts  774 us (83%)
  other arithmetic  71.9 us (8%)
  starting transfers between devices  44 us (5%)
  waiting for transfers between devices  17.8 us (2%)
  blocking collectives  13.4 us (1%)
    gather x32, local copies, waits for them, and re-layouts, group_pull(): picked = essential[:, particle_ids]  592 us
    gather x32, local copies, waits for them, and re-layouts, group_pull(): moments = cell_table[:, cell_ids]  140 us
    ppermute x8, starting transfers between devices, passed_along(): lax.ppermute(value, axis, [(source, source + steps) for source in range(l...  26.5 us
    while x2, local copies, waits for them, and re-layouts, on_device(): pulled = lax.map(one_block, (target_blocks, leaf_blocks, cell_blocks))  18.8 us
  transfers between devices with their start and end apart: 9, of which 4 were waited for; matrix products, arithmetic and copies ran while one was open for 1% of the time, Pallas kernels for 0%

profile of v1, /device:TPU:1, one launch (start us, length us, event | category | flops | bytes accessed | tf_op | source)
XLA Modules:
  0.0 924.1 jit_solution(10534818323463038066)
XLA Ops:
  4.0 12.9 %gather_fusion.2 = f32[4096,4]{1,0:T(8,128)S(1)} fusion(f32[4,8192]{0,1:T(8,128)} %copy.59, s32[4096]{0:T(1024)S(1)} %broadcast_clamp_fusion), kind=kCustom, calls=%fused_computation.2 | custom fusion | bytes 147456 | tf_op jit(solution)/shard_map/gather | solution.py:87
  32.6 17.5 %all-to-all-start = ((f32[256,10,128]{2,1,0:T(8,128)}), f32[256,10,128]{2,1,0:T(8,128)S(1)}, u32[]{:S(2)}, u32[]{:S(2)}) async-start(f32[256,10,128]{2,1,0:T(8,128)} %stack.31), calls=%async_computation | async-start | bytes 4194304 | tf_op jit(solution)/shard_map/all_to_all | solution.py:73
  63.4 13.4 %all_gather.3 = f32[4,32768]{1,0:T(4,128)S(1)} all-gather(f32[4,8192]{1,0:T(4,128)S(1)} %pad_maximum_fusion.2), channel_id=1, replica_groups=mesh['dom'=64,'sub'=4] {'sub'}, dimensions={1}, use_global_device_ids=true | all-gather | bytes 655360 | tf_op jit(solution)/shard_map/all_gather | solution.py:79
  77.1 9.0 collective-permute-done.5
  86.9 9.8 %copy.69 = f32[4,36864]{0,1:T(8,128)} copy(f32[4,36864]{1,0:T(4,128)S(1)} %pad_maximum_fusion.1) | data formatting | bytes 1179648 | tf_op jit(solution)/shard_map/while | solution.py:103
  105.0 9.0 copy.73
  114.0 809.3 %while.10 = (s32[]{:T(128)}, f32[16,3,8,64]{3,2,1,0:T(8,128)S(1)}, s32[16,8,16]{2,1,0:T(8,128)S(1)}, f32[4,36864]{0,1:T(8,128)}, f32[16,3,8,64]{3,2,0,1:T(8,128)...) while((s32[]{:T(128)}, f32[16,3,8,64]{3,2,1,0:T(8,128)S(1)}, s32[16,8,16]{2,1,0:T(8,128)S(1)}, ...), condition=%wide.region_6.7_spmd, body=%wide.region_0.6_spmd.sunk | while | flops 15249026 | bytes 16653933 | solution.py:103
  114.3 34.1 %gather_fusion = f32[8192,4]{1,0:T(8,128)} fusion(f32[4,36864]{0,1:T(8,128)} %get-tuple-element.200, s32[8192]{0:T(1024)S(1)} %bitcast_clamp_fusion.2), kind=kCustom, calls=%fused_computation.clone.1 | custom fusion | bytes 294912 | tf_op jit(solution)/shard_map/while/body/eval_jaxpr/gather | solution.py:54
  164.9 34.1 %gather_fusion = f32[8192,4]{1,0:T(8,128)} fusion(f32[4,36864]{0,1:T(8,128)} %get-tuple-element.200, s32[8192]{0:T(1024)S(1)} %bitcast_clamp_fusion.2), kind=kCustom, calls=%fused_computation.clone.1 | custom fusion | bytes 294912 | tf_op jit(solution)/shard_map/while/body/eval_jaxpr/gather | solution.py:54
  215.5 34.1 %gather_fusion = f32[8192,4]{1,0:T(8,128)} fusion(f32[4,36864]{0,1:T(8,128)} %get-tuple-element.200, s32[8192]{0:T(1024)S(1)} %bitcast_clamp_fusion.2), kind=kCustom, calls=%fused_computation.clone.1 | custom fusion | bytes 294912 | tf_op jit(solution)/shard_map/while/body/eval_jaxpr/gather | solution.py:54
  266.0 34.1 %gather_fusion = f32[8192,4]{1,0:T(8,128)} fusion(f32[4,36864]{0,1:T(8,128)} %get-tuple-element.200, s32[8192]{0:T(1024)S(1)} %bitcast_clamp_fusion.2), kind=kCustom, calls=%fused_computation.clone.1 | custom fusion | bytes 294912 | tf_op jit(solution)/shard_map/while/body/eval_jaxpr/gather | solution.py:54
  316.6 34.1 %gather_fusion = f32[8192,4]{1,0:T(8,128)} fusion(f32[4,36864]{0,1:T(8,128)} %get-tuple-element.200, s32[8192]{0:T(1024)S(1)} %bitcast_clamp_fusion.2), kind=kCustom, calls=%fused_computation.clone.1 | custom fusion | bytes 294912 | tf_op jit(solution)/shard_map/while/body/eval_jaxpr/gather | solution.py:54
  367.2 34.1 %gather_fusion = f32[8192,4]{1,0:T(8,128)} fusion(f32[4,36864]{0,1:T(8,128)} %get-tuple-element.200, s32[8192]{0:T(1024)S(1)} %bitcast_clamp_fusion.2), kind=kCustom, calls=%fused_computation.clone.1 | custom fusion | bytes 294912 | tf_op jit(solution)/shard_map/while/body/eval_jaxpr/gather | solution.py:54
  407.3 8.6 gather_fusion.1
  417.8 34.1 %gather_fusion = f32[8192,4]{1,0:T(8,128)} fusion(f32[4,36864]{0,1:T(8,128)} %get-tuple-element.200, s32[8192]{0:T(1024)S(1)} %bitcast_clamp_fusion.2), kind=kCustom, calls=%fused_computation.clone.1 | custom fusion | bytes 294912 | tf_op jit(solution)/shard_map/while/body/eval_jaxpr/gather | solution.py:54
  468.4 34.1 %gather_fusion = f32[8192,4]{1,0:T(8,128)} fusion(f32[4,36864]{0,1:T(8,128)} %get-tuple-element.200, s32[8192]{0:T(1024)S(1)} %bitcast_clamp_fusion.2), kind=kCustom, calls=%fused_computation.clone.1 | custom fusion | bytes 294912 | tf_op jit(solution)/shard_map/while/body/eval_jaxpr/gather | solution.py:54
  518.9 34.1 %gather_fusion = f32[8192,4]{1,0:T(8,128)} fusion(f32[4,36864]{0,1:T(8,128)} %get-tuple-element.200, s32[8192]{0:T(1024)S(1)} %bitcast_clamp_fusion.2), kind=kCustom, calls=%fused_computation.clone.1 | custom fusion | bytes 294912 | tf_op jit(solution)/shard_map/while/body/eval_jaxpr/gather | solution.py:54
  569.5 34.1 %gather_fusion = f32[8192,4]{1,0:T(8,128)} fusion(f32[4,36864]{0,1:T(8,128)} %get-tuple-element.200, s32[8192]{0:T(1024)S(1)} %bitcast_clamp_fusion.2), kind=kCustom, calls=%fused_computation.clone.1 | custom fusion | bytes 294912 | tf_op jit(solution)/shard_map/while/body/eval_jaxpr/gather | solution.py:54
  620.1 34.1 %gather_fusion = f32[8192,4]{1,0:T(8,128)} fusion(f32[4,36864]{0,1:T(8,128)} %get-tuple-element.200, s32[8192]{0:T(1024)S(1)} %bitcast_clamp_fusion.2), kind=kCustom, calls=%fused_computation.clone.1 | custom fusion | bytes 294912 | tf_op jit(solution)/shard_map/while/body/eval_jaxpr/gather | solution.py:54
  670.7 34.1 %gather_fusion = f32[8192,4]{1,0:T(8,128)} fusion(f32[4,36864]{0,1:T(8,128)} %get-tuple-element.200, s32[8192]{0:T(1024)S(1)} %bitcast_clamp_fusion.2), kind=kCustom, calls=%fused_computation.clone.1 | custom fusion | bytes 294912 | tf_op jit(solution)/shard_map/while/body/eval_jaxpr/gather | solution.py:54
  721.3 34.1 %gather_fusion = f32[8192,4]{1,0:T(8,128)} fusion(f32[4,36864]{0,1:T(8,128)} %get-tuple-element.200, s32[8192]{0:T(1024)S(1)} %bitcast_clamp_fusion.2), kind=kCustom, calls=%fused_computation.clone.1 | custom fusion | bytes 294912 | tf_op jit(solution)/shard_map/while/body/eval_jaxpr/gather | solution.py:54
  771.9 34.1 %gather_fusion = f32[8192,4]{1,0:T(8,128)} fusion(f32[4,36864]{0,1:T(8,128)} %get-tuple-element.200, s32[8192]{0:T(1024)S(1)} %bitcast_clamp_fusion.2), kind=kCustom, calls=%fused_computation.clone.1 | custom fusion | bytes 294912 | tf_op jit(solution)/shard_map/while/body/eval_jaxpr/gather | solution.py:54
  822.4 34.1 %gather_fusion = f32[8192,4]{1,0:T(8,128)} fusion(f32[4,36864]{0,1:T(8,128)} %get-tuple-element.200, s32[8192]{0:T(1024)S(1)} %bitcast_clamp_fusion.2), kind=kCustom, calls=%fused_computation.clone.1 | custom fusion | bytes 294912 | tf_op jit(solution)/shard_map/while/body/eval_jaxpr/gather | solution.py:54
  873.0 34.1 %gather_fusion = f32[8192,4]{1,0:T(8,128)} fusion(f32[4,36864]{0,1:T(8,128)} %get-tuple-element.200, s32[8192]{0:T(1024)S(1)} %bitcast_clamp_fusion.2), kind=kCustom, calls=%fused_computation.clone.1 | custom fusion | bytes 294912 | tf_op jit(solution)/shard_map/while/body/eval_jaxpr/gather | solution.py:54
  (465 shorter events, 295.0 us)
Async XLA Ops:
  0.0 3.7 copy-start.3
  0.0 17.6 %copy-start.6 = (s32[1,1,8]{2,1,0:T(1,128)S(1)}, s32[1,1,8]{2,1,0:T(1,128)}, u32[]{:S(2)}) copy-start(s32[1,1,8]{2,1,0:T(1,128)} %param.19) | copy-start | bytes 100
  0.0 31.1 %copy-start.4 = (f32[6,128]{1,0:T(8,128)S(1)}, f32[6,128]{1,0:T(8,128)}, u32[]{:S(2)}) copy-start(f32[6,128]{1,0:T(8,128)} %param.15) | copy-start | bytes 9220
  0.0 31.1 %copy-start.5 = (f32[3,128]{1,0:T(4,128)S(1)}, f32[3,128]{1,0:T(4,128)}, u32[]{:S(2)}) copy-start(f32[3,128]{1,0:T(4,128)} %param.14) | copy-start | bytes 4612
  0.0 31.1 %copy-start.7 = (f32[128]{0:T(128)S(1)}, f32[128]{0:T(128)}, u32[]{:S(2)}) copy-start(f32[128]{0:T(128)} %param.13) | copy-start | bytes 1540
  17.6 59.2 %copy-start = (f32[3,8192]{1,0:T(4,128)S(1)}, f32[3,8192]{1,0:T(4,128)}, u32[]{:S(2)}) copy-start(f32[3,8192]{1,0:T(4,128)} %param.11) | copy-start | bytes 294916
  17.6 59.4 %copy-start.2 = (s32[128,16]{0,1:T(8,128)S(1)}, s32[128,16]{0,1:T(8,128)}, u32[]{:S(2)}) copy-start(s32[128,16]{0,1:T(8,128)} %param.17) | copy-start | bytes 24580
  17.8 32.2 %collective-permute-start = (f32[4,512]{1,0:T(4,128)S(1)}, f32[4,512]{1,0:T(4,128)S(1)}, u32[]{:S(2)}, u32[]{:S(2)}) collective-permute-start(f32[4,512]{1,0:T(4,128)S(1)} %get-tuple-element.107), channel_id=1, source_target_pairs={{16,0},{20,4},{24,8},{28,12},{32,16},{36,20},{40,24},{44,28},{48,3... | collective-permute-start | bytes 24584 | tf_op jit(solution)/shard_map/ppermute | solution.py:18
  19.1 34.3 %collective-permute-start.1 = (f32[4,512]{1,0:T(4,128)S(1)}, f32[4,512]{1,0:T(4,128)S(1)}, u32[]{:S(2)}, u32[]{:S(2)}) collective-permute-start(f32[4,512]{1,0:T(4,128)S(1)} %get-tuple-element.106), channel_id=1, source_target_pairs={{12,0},{16,4},{20,8},{24,12},{28,16},{32,20},{36,24},{40,28},{44,3... | collective-permute-start | bytes 24584 | tf_op jit(solution)/shard_map/ppermute | solution.py:18
  20.4 38.1 %collective-permute-start.2 = (f32[4,512]{1,0:T(4,128)S(1)}, f32[4,512]{1,0:T(4,128)S(1)}, u32[]{:S(2)}, u32[]{:S(2)}) collective-permute-start(f32[4,512]{1,0:T(4,128)S(1)} %get-tuple-element.105), channel_id=1, source_target_pairs={{8,0},{12,4},{16,8},{20,12},{24,16},{28,20},{32,24},{36,28},{40,32... | collective-permute-start | bytes 24584 | tf_op jit(solution)/shard_map/ppermute | solution.py:18
  21.7 55.3 %collective-permute-start.3 = (f32[4,512]{1,0:T(4,128)S(1)}, f32[4,512]{1,0:T(4,128)S(1)}, u32[]{:S(2)}, u32[]{:S(2)}) collective-permute-start(f32[4,512]{1,0:T(4,128)S(1)} %get-tuple-element.104), channel_id=1, source_target_pairs={{4,0},{8,4},{12,8},{16,12},{20,16},{24,20},{28,24},{32,28},{36,32}... | collective-permute-start | bytes 24584 | tf_op jit(solution)/shard_map/ppermute | solution.py:18
  26.9 50.2 %collective-permute-start.4 = (f32[4,512]{1,0:T(4,128)S(1)}, f32[4,512]{1,0:T(4,128)S(1)}, u32[]{:S(2)}, u32[]{:S(2)}) collective-permute-start(f32[4,512]{1,0:T(4,128)S(1)} %get-tuple-element.103), channel_id=1, source_target_pairs={{0,4},{4,8},{8,12},{12,16},{16,20},{20,24},{24,28},{28,32},{32,36}... | collective-permute-start | bytes 24584 | tf_op jit(solution)/shard_map/ppermute | solution.py:18
  32.6 72.5 %all-to-all-start = ((f32[256,10,128]{2,1,0:T(8,128)}), f32[256,10,128]{2,1,0:T(8,128)S(1)}, u32[]{:S(2)}, u32[]{:S(2)}) async-start(f32[256,10,128]{2,1,0:T(8,128)} %stack.31), calls=%async_computation | async-start | bytes 4194304 | tf_op jit(solution)/shard_map/all_to_all | solution.py:73
  50.0 36.1 %collective-permute-start.5 = (f32[4,512]{1,0:T(4,128)S(1)}, f32[4,512]{1,0:T(4,128)S(1)}, u32[]{:S(2)}, u32[]{:S(2)}) collective-permute-start(f32[4,512]{1,0:T(4,128)S(1)} %get-tuple-element.102), channel_id=1, source_target_pairs={{0,8},{4,12},{8,16},{12,20},{16,24},{20,28},{24,32},{28,36},{32,40... | collective-permute-start | bytes 24584 | tf_op jit(solution)/shard_map/ppermute | solution.py:18
  53.5 32.9 %collective-permute-start.6 = (f32[4,512]{1,0:T(4,128)S(1)}, f32[4,512]{1,0:T(4,128)S(1)}, u32[]{:S(2)}, u32[]{:S(2)}) collective-permute-start(f32[4,512]{1,0:T(4,128)S(1)} %get-tuple-element.101), channel_id=1, source_target_pairs={{0,12},{4,16},{8,20},{12,24},{16,28},{20,32},{24,36},{28,40},{32,4... | collective-permute-start | bytes 24584 | tf_op jit(solution)/shard_map/ppermute | solution.py:18
  58.5 28.1 %collective-permute-start.7 = (f32[4,512]{1,0:T(4,128)S(1)}, f32[4,512]{1,0:T(4,128)S(1)}, u32[]{:S(2)}, u32[]{:S(2)}) collective-permute-start(f32[4,512]{1,0:T(4,128)S(1)} %get-tuple-element.100), channel_id=1, source_target_pairs={{0,16},{4,20},{8,24},{12,28},{16,32},{20,36},{24,40},{28,44},{32,4... | collective-permute-start | bytes 24584 | tf_op jit(solution)/shard_map/ppermute | solution.py:18
  105.0 9.0 copy-start.1
